TPU v7x, 32 devices: a whole 2x2x4 slice. The times are simulated.
32 devices in a mesh: blk: 16 (over z, y, x), grp: 2 (over core).
Axes of the slice: x: 2, y: 2, z: 4, core: 2. Of those that a mesh axis runs over, the one named last changes fastest.
Arguments:
- image_emb: bfloat16 [4096, 1152], P(('blk', 'grp')), may hold values from -6 to 6
- text_feats: bfloat16 [4096, 640], P(('blk', 'grp')), may hold values from -6 to 6
- text_head: bfloat16 [640, 1152], replicated, may hold values from -0.25 to 0.25
Outputs:
- row_loss: float32 [4096], P(('blk', 'grp'))
- head_grad: float32 [640, 1152], P('blk')
All inputs are finite; a program needn't handle non-finite values.
Results may differ from a plain program's by a relative error of at most 0.0053.
Values may be sent and summed in bfloat16 or wider, within the bound.
A program may use at most 64 MiB of HBM per device.

v0:
```python
import jax
import jax.numpy as jnp
from jax import lax
from jax.sharding import PartitionSpec as P

STEPS = 2


logit_scale = 20.0
logit_bias = -2.0
eps_norm = 1e-06


def shifted(block, axis, distance):
    devices = range(lax.axis_size(axis))
    route = [((i - distance) % len(devices), i) for i in devices]
    return lax.ppermute(block, axis, route)


def per_device(image_emb, text_feats, text_head):
    tok_rows = image_emb.shape[0]
    image_wide = image_emb.astype(jnp.float32)
    inverse = lax.rsqrt(jnp.sum(image_wide * image_wide, axis=1, keepdims=True) + eps_norm)
    images = (image_wide * inverse).astype(jnp.bfloat16)
    projected = jnp.dot(text_feats, text_head, preferred_element_type=jnp.float32)
    radius = jnp.sqrt(jnp.sum(projected * projected, axis=1, keepdims=True) + eps_norm)
    text_units = (projected / radius).astype(jnp.bfloat16)
    pair_count = (STEPS + 1) * tok_rows
    identity = jnp.eye(tok_rows, dtype=jnp.float32)
    negative = -jnp.ones((tok_rows, tok_rows), jnp.float32)

    def meet_span(image_rows, visitor, pair_sign):
        scores = (
            logit_scale
            * jnp.einsum("ie,je->ij", image_rows, visitor, preferred_element_type=jnp.float32)
            + logit_bias
        )
        margin_arg = -pair_sign * scores
        loss_part = jnp.sum(jax.nn.softplus(margin_arg), axis=1) / pair_count
        pair_weight = (-pair_sign * jax.nn.sigmoid(margin_arg) * (logit_scale / pair_count)).astype(
            jnp.bfloat16
        )
        partial_grad = jnp.einsum(
            "ij,ie->je", pair_weight, image_rows, preferred_element_type=jnp.float32
        )
        return (loss_part, partial_grad)

    row_loss, grad_text = meet_span(images, text_units, 2.0 * identity - 1.0)
    visitor = text_units
    carried = grad_text
    for hop_count in range(STEPS):
        visitor = shifted(visitor, "blk", 1)
        carried = shifted(carried, "blk", 1)
        loss_part, partial_grad = meet_span(images, visitor, negative)
        row_loss = row_loss + loss_part
        carried = carried + partial_grad
    grad_text = shifted(carried, "blk", -STEPS)
    along = jnp.sum(projected * grad_text, axis=1, keepdims=True)
    grad_proj = (grad_text / radius - projected * (along / (radius * radius * radius))).astype(
        jnp.bfloat16
    )
    local_grad = jnp.einsum("td,te->de", text_feats, grad_proj, preferred_element_type=jnp.float32)
    row_sums = lax.psum_scatter(local_grad, "blk", scatter_dimension=0, tiled=True)
    head_grad = lax.psum(row_sums, "grp")
    return (row_loss, head_grad)


def solution(mesh):
    placed = (P(("blk", "grp"), None), P(("blk", "grp"), None), P())
    return jax.shard_map(
        per_device,
        mesh=mesh,
        in_specs=placed,
        out_specs=(P(("blk", "grp")), P("blk", None)),
        check_vma=False,
    )
```

profile of v0, /device:TPU:0, one launch (start us, length us, event | category | flops | bytes accessed | tf_op | source)
XLA Modules:
  0.0 250.5 jit_solution(9647802244620505869)
XLA Ops:
  7.2 1.3 copy-done
  8.5 1.4 multiply_reduce_fusion.1
  10.0 1.1 fusion.4
  11.2 0.4 fusion.8
  11.6 0.3 fusion.11
  12.0 3.0 %collective-permute-start.2 = (f32[128,1152]{1,0:T(8,128)S(1)}, f32[128,1152]{1,0:T(8,128)S(1)}, u32[]{:S(2)}, u32[]{:S(2)}) collective-permute-start(f32[128,1152]{1,0:T(8,128)S(1)} %fusion.11), channel_id=1, source_target_pairs={{30,0},{0,2},{2,4},{4,6},{6,8},{8,10},{10,12},{12,14},{14,16},{16,... | collective-permute-start | bytes 1769480 | tf_op jit(solution)/shard_map/ppermute | solution.py:17
  14.9 1.5 collective-permute-start
  16.4 22.1 %collective-permute-done = bf16[128,1152]{1,0:T(8,128)(2,1)S(1)} collective-permute-done((bf16[128,1152]{1,0:T(8,128)(2,1)S(1)}, bf16[128,1152]{1,0:T(8,128)(2,1)S(1)}, u32[]{:S(2)}, u32[]{:S(2)}) %collective-permute-start) | collective-permute-done | bytes 294944 | tf_op jit(solution)/shard_map/ppermute | solution.py:17
  38.6 0.4 fusion.9
  39.0 0.3 convolution_add_fusion
  39.3 0.2 collective-permute-start.3
  39.5 12.6 %collective-permute-done.1 = bf16[128,1152]{1,0:T(8,128)(2,1)S(1)} collective-permute-done((bf16[128,1152]{1,0:T(8,128)(2,1)S(1)}, bf16[128,1152]{1,0:T(8,128)(2,1)S(1)}, u32[]{:S(2)}, u32[]{:S(2)}) %collective-permute-start.1) | collective-permute-done | bytes 294944 | tf_op jit(solution)/shard_map/ppermute | solution.py:17
  52.1 0.4 fusion.10
  52.5 0.3 fusion.12
  52.8 10.2 %collective-permute-done.3 = f32[128,1152]{1,0:T(8,128)S(1)} collective-permute-done((f32[128,1152]{1,0:T(8,128)S(1)}, f32[128,1152]{1,0:T(8,128)S(1)}, u32[]{:S(2)}, u32[]{:S(2)}) %collective-permute-start.3) | collective-permute-done | bytes 589856 | tf_op jit(solution)/shard_map/ppermute | solution.py:17
  63.1 13.6 %collective-permute-done.4 = f32[128,1152]{1,0:T(8,128)S(1)} collective-permute-done((f32[128,1152]{1,0:T(8,128)S(1)}, f32[128,1152]{1,0:T(8,128)S(1)}, u32[]{:S(2)}, u32[]{:S(2)}) %collective-permute-start.4) | collective-permute-done | bytes 589856 | tf_op jit(solution)/shard_map/ppermute | solution.py:17
  76.7 0.1 multiply_reduce_fusion
  76.8 2.3 convolution_bitcast_fusion
  79.2 0.6 dynamic-slice
  80.5 140.8 %all-reduce.6.cloned.1.call-done = f32[640,1152]{0,1:T(8,128)} async-done(((f32[640,1152]{0,1:T(8,128)}), f32[640,1152]{0,1:T(8,128)}) %all-reduce.6.cloned.1.call-update) | async-done | bytes 2949136
  221.2 2.3 constant_dynamic-slice_fusion
  223.6 0.5 add_multiply_fusion
  224.1 17.6 %all-reduce.4.cloned.1.call-done = f32[40,1152]{0,1:T(8,128)} async-done(((f32[40,1152]{0,1:T(8,128)}), f32[40,1152]{0,1:T(8,128)}) %all-reduce.4.cloned.1.call-update) | async-done | bytes 184336 | tf_op jit(solution)/shard_map/psum | solution.py:64
  241.7 1.9 copy.6
  (19 shorter events, 0.4 us)
Async XLA Ops:
  7.2 1.4 copy-start
  7.2 4.1 %copy-start.1 = (bf16[128,1152]{1,0:T(8,128)(2,1)S(1)}, bf16[128,1152]{1,0:T(8,128)(2,1)}, u32[]{:S(2)}) copy-start(bf16[128,1152]{1,0:T(8,128)(2,1)} %param.3) | copy-start | bytes 884740
  7.2 214.0 %all-reduce.6.cloned.1.call-start = ((), (), s32[]{:S(2)}) async-start(), calls=%async_computation.1 | async-start | bytes 5898240
  12.0 27.0 %collective-permute-start.2 = (f32[128,1152]{1,0:T(8,128)S(1)}, f32[128,1152]{1,0:T(8,128)S(1)}, u32[]{:S(2)}, u32[]{:S(2)}) collective-permute-start(f32[128,1152]{1,0:T(8,128)S(1)} %fusion.11), channel_id=1, source_target_pairs={{30,0},{0,2},{2,4},{4,6},{6,8},{8,10},{10,12},{12,14},{14,16},{16,... | collective-permute-start | bytes 1769480 | tf_op jit(solution)/shard_map/ppermute | solution.py:17
  14.9 23.6 %collective-permute-start = (bf16[128,1152]{1,0:T(8,128)(2,1)S(1)}, bf16[128,1152]{1,0:T(8,128)(2,1)S(1)}, u32[]{:S(2)}, u32[]{:S(2)}) collective-permute-start(bf16[128,1152]{1,0:T(8,128)(2,1)S(1)} %divide_convert_fusion), channel_id=1, source_target_pairs={{30,0},{0,2},{2,4},{4,6},{6,8},{8,10},{10,12},{12,14},{14,16},{16,... | collective-permute-start | bytes 884744 | tf_op jit(solution)/shard_map/ppermute | solution.py:17
  38.6 13.5 %collective-permute-start.1 = (bf16[128,1152]{1,0:T(8,128)(2,1)S(1)}, bf16[128,1152]{1,0:T(8,128)(2,1)S(1)}, u32[]{:S(2)}, u32[]{:S(2)}) collective-permute-start(bf16[128,1152]{1,0:T(8,128)(2,1)S(1)} %collective-permute-done), channel_id=1, source_target_pairs={{30,0},{0,2},{2,4},{4,6},{6,8},{8,10},{10,12},{12,14},{14,16},{16,... | collective-permute-start | bytes 884744 | tf_op jit(solution)/shard_map/ppermute | solution.py:17
  39.0 37.9 %copy-start.2 = (bf16[128,640]{1,0:T(8,128)(2,1)S(1)}, bf16[128,640]{1,0:T(8,128)(2,1)}, u32[]{:S(2)}) copy-start(bf16[128,640]{1,0:T(8,128)(2,1)} %param.4) | copy-start | bytes 491524
  39.3 23.7 %collective-permute-start.3 = (f32[128,1152]{1,0:T(8,128)S(1)}, f32[128,1152]{1,0:T(8,128)S(1)}, u32[]{:S(2)}, u32[]{:S(2)}) collective-permute-start(f32[128,1152]{1,0:T(8,128)S(1)} %convolution_add_fusion), channel_id=1, source_target_pairs={{30,0},{0,2},{2,4},{4,6},{6,8},{8,10},{10,12},{12,14},{14,16},{16,... | collective-permute-start | bytes 1769480 | tf_op jit(solution)/shard_map/ppermute | solution.py:17
  63.1 13.6 %collective-permute-start.4 = (f32[128,1152]{1,0:T(8,128)S(1)}, f32[128,1152]{1,0:T(8,128)S(1)}, u32[]{:S(2)}, u32[]{:S(2)}) collective-permute-start(f32[128,1152]{1,0:T(8,128)S(1)} %add.78), channel_id=1, source_target_pairs={{4,0},{6,2},{8,4},{10,6},{12,8},{14,10},{16,12},{18,14},{20,16},{2... | collective-permute-start | bytes 1769480 | tf_op jit(solution)/shard_map/ppermute | solution.py:17
  76.8 2.4 copy-start.3
  79.2 162.5 %all-reduce.4.cloned.1.call-start = ((), (), s32[]{:S(2)}) async-start(), calls=%async_computation | async-start | bytes 1179648 | tf_op jit(solution)/shard_map/psum | solution.py:64
Sparse Core Ops, SparseCore 0:
  79.3 141.8 all-reduce.5
  223.7 17.9 all-reduce.3
where the time goes:
time: 251 us
  waiting for transfers between devices  217 us (86%)
  between operations  14.8 us (6%)
  local copies, waits for them, and re-layouts  6.17 us (2%)
  matrix products  5.82 us (2%)
  starting transfers between devices  4.82 us (2%)
    unnamed x3, waiting for transfers between devices  141 us
    ppermute x5, waiting for transfers between devices, shifted(): return lax.ppermute(block, axis, route)  58.5 us
    psum x1, waiting for transfers between devices, per_device(): head_grad = lax.psum(row_sums, 'grp')  17.6 us
    unnamed x11, local copies, waits for them, and re-layouts  6.17 us
  transfers between devices with their start and end apart: 7, of which 6 were waited for; matrix products, arithmetic and copies ran while one was open for 1% of the time, Pallas kernels for 0%

commit v1 on v0

v1 whole, which is shorter than its diff:
```python
import functools

import jax
import jax.numpy as jnp
from jax import lax
from jax.experimental import pallas as pl
from jax.experimental.pallas import tpu as pltpu
from jax.sharding import PartitionSpec as P

STEPS = 2
MESH = pl.DeviceIdType.MESH

logit_scale = 20.0
logit_bias = -2.0
eps_norm = 1e-06

LANES = 128
N_CHUNK = 4
ORDERS = ((0, 1, 2, 3), (1, 2, 0, 3), (2, 0, 1, 3))


def position(order, dest):
    place = 0
    for bit in order:
        place = 2 * place + (dest >> bit) % 2
    return place


def unit_images(image_emb):
    wide = image_emb.astype(jnp.float32)
    inverse = lax.rsqrt(jnp.sum(wide * wide, axis=1, keepdims=True) + eps_norm)
    return (wide * inverse).astype(jnp.bfloat16)


def meet(images, feats, head, own):
    tok = images.shape[0]
    pairs = (STEPS + 1) * tok
    projected = jnp.dot(feats, head, preferred_element_type=jnp.float32)
    inverse = lax.rsqrt(jnp.sum(projected * projected, axis=1, keepdims=True) + eps_norm)
    texts = (projected * inverse).astype(jnp.bfloat16)
    scores = (
        logit_scale
        * lax.dot_general(texts, images, (((1,), (1,)), ((), ())), preferred_element_type=jnp.float32)
        + logit_bias
    )
    if own:
        same = lax.broadcasted_iota(jnp.int32, (tok, tok), 0) == lax.broadcasted_iota(
            jnp.int32, (tok, tok), 1
        )
        minus_sign = jnp.where(same, -1.0, 1.0)
        arg = minus_sign * scores
    else:
        arg = scores
    small = jnp.exp(-jnp.abs(arg))
    loss = jnp.sum(jnp.maximum(arg, 0.0) + jnp.log1p(small), axis=0, keepdims=True) / pairs
    weight = jnp.where(arg >= 0, 1.0, small) / (1.0 + small) * (logit_scale / pairs)
    if own:
        weight = minus_sign * weight
    grad = jnp.dot(weight.astype(jnp.bfloat16), images, preferred_element_type=jnp.float32)
    along = jnp.sum(projected * grad, axis=1, keepdims=True)
    grad_proj = inverse * (grad - projected * (along * inverse * inverse))
    return loss, grad_proj.astype(jnp.bfloat16)


def kernel(
    n_blk, image_hbm, feats_hbm, head_hbm, loss_ref, out_ref,
    image_v, head_v, units, feats, feats_t, grads, total, core_out, core_in,
    out0, out1, out2, out3, in0, in1, in2, in3, mine, theirs,
    load_sem, s1, r1, s2, r2, core_s, core_r, step_s, step_r, last_s, last_r,
):
    blk, grp = lax.axis_index("blk"), lax.axis_index("grp")
    parity = lax.rem(blk, 2)

    def flipped(bit):
        size = 1 << bit
        return blk + size * (1 - 2 * lax.rem(blk // size, 2))

    pair = (flipped(0), grp)
    ahead = (lax.rem(blk + 2, n_blk), grp)
    behind = (lax.rem(blk + n_blk - 2, n_blk), grp)
    other = (blk, 1 - grp)
    partners = [(flipped(bit), grp) for bit in range(4)]

    loads = [
        pltpu.make_async_copy(src, dst, load_sem.at[n])
        for n, (src, dst) in enumerate(((image_hbm, image_v), (feats_hbm, feats.at[0]), (head_hbm, head_v)))
    ]
    for load in loads:
        load.start()

    barrier = pltpu.get_barrier_semaphore()
    greeted = partners + [ahead, behind, other]
    for device in greeted:
        pl.semaphore_signal(barrier, inc=1, device_id=device, device_id_type=MESH)
    pl.semaphore_wait(barrier, len(greeted))

    def remote(src, dst, send, recv, device):
        return pltpu.make_async_remote_copy(
            src_ref=src, dst_ref=dst, send_sem=send, recv_sem=recv, device_id=device, device_id_type=MESH
        )

    rows = feats.shape[1] // N_CHUNK
    spans = [pl.ds(c * rows, rows) for c in range(N_CHUNK)]
    far = [
        remote(feats_hbm.at[w], feats.at[2, w], s2.at[c], r2.at[c], ahead) for c, w in enumerate(spans)
    ]
    near = [
        remote(feats_hbm.at[w], feats.at[1, w], s1.at[c], r1.at[c], pair) for c, w in enumerate(spans)
    ]
    onward = [
        remote(feats.at[2, w], feats.at[1, w], s1.at[c], r1.at[c], pair) for c, w in enumerate(spans)
    ]
    for copy in far:
        copy.start()

    @pl.when(parity == 0)
    def _():
        for copy in near:
            copy.start()

    loads[0].wait()
    units[...] = unit_images(image_v[...])
    loads[1].wait()
    loads[2].wait()

    tok = units.shape[0]

    def block(k):
        loss, grad = meet(units[...], feats[k], head_v[...], k == 0)
        grads[k * tok : (k + 1) * tok, :] = grad
        feats_t[:, k * tok : (k + 1) * tok] = feats[k].T
        return loss

    loss = block(0)

    for c in range(N_CHUNK):
        far[c].wait_recv()

        @pl.when(parity == 1)
        def _():
            onward[c].start()

    loss = loss + block(2)
    for copy in near:
        copy.wait_recv()
    loss_ref[...] = loss + block(1)

    depth = out_ref.shape[0]
    width = total.shape[2]
    columns = out_ref.shape[1] // len(ORDERS)
    tiles = columns // LANES
    full = depth * tiles
    first = grp == 0

    core_copies = [
        remote(core_out.at[p], core_in.at[p], core_s.at[p], core_r.at[p], other) for p in range(len(ORDERS))
    ]

    def products(p):
        grad = jnp.dot(
            feats_t[...], grads[:, p * columns : (p + 1) * columns], preferred_element_type=jnp.float32
        )
        for dest in range(n_blk):
            piece = grad[dest * depth : (dest + 1) * depth]
            stack = jnp.concatenate([piece[:, t * LANES : (t + 1) * LANES] for t in range(tiles)], axis=0)
            low, high = stack[:width], stack[full - width :]
            at = position(ORDERS[p], dest)
            total[p, at] = jnp.where(first, low, high)
            core_out[p, at] = jnp.where(first, high, low).astype(jnp.bfloat16)
        core_copies[p].start()

    outs, ins = (out0, out1, out2, out3), (in0, in1, in2, in3)
    step_copies = [
        [
            remote(outs[s].at[p], ins[s].at[p], step_s.at[p, s], step_r.at[p, s], partners[ORDERS[p][s]])
            for s in range(4)
        ]
        for p in range(len(ORDERS))
    ]
    base = [0] * len(ORDERS)

    def halve(p, s):
        count = n_blk >> (s + 1)
        bit = lax.rem(blk // (1 << ORDERS[p][s]), 2)
        keep, give = base[p] + bit * count, base[p] + (1 - bit) * count
        if s == 0:
            core_copies[p].wait_recv()
            arrived, start = core_in, 0
        else:
            step_copies[p][s - 1].wait_recv()
            arrived, start = ins[s - 1], base[p]
        gone = pl.ds(give, count)
        outs[s][p] = (total[p, gone] + arrived[p, pl.ds(give - start, count)].astype(jnp.float32)).astype(
            jnp.bfloat16
        )
        step_copies[p][s].start()
        stay = pl.ds(keep, count)
        total[p, stay] = total[p, stay] + arrived[p, pl.ds(keep - start, count)].astype(jnp.float32)
        base[p] = keep

    products(0)
    products(1)
    halve(0, 0)
    products(2)
    halve(1, 0)
    halve(2, 0)
    for s in range(1, 4):
        for p in range(len(ORDERS)):
            halve(p, s)
    for p in range(len(ORDERS)):
        step_copies[p][3].wait_recv()
        mine[p] = total[p, base[p]] + in3[p, 0].astype(jnp.float32)
    last = remote(mine, theirs, last_s, last_r, other)
    last.start()
    last.wait_recv()
    for p in range(len(ORDERS)):
        here, there = mine[p], theirs[p]
        low, high = jnp.where(first, here, there), jnp.where(first, there, here)
        stack = jnp.concatenate([low[: full - width], high], axis=0)
        for t in range(tiles):
            left = p * columns + t * LANES
            out_ref[:, left : left + LANES] = stack[t * depth : (t + 1) * depth]

    last.wait_send()
    for copy in far + near + core_copies:
        copy.wait_send()
    for chain in step_copies:
        for copy in chain:
            copy.wait_send()


def fused(n_blk, image_emb, text_feats, text_head):
    tok, emb = image_emb.shape
    feat = text_feats.shape[1]
    depth = feat // n_blk
    parts = len(ORDERS)
    full = depth * (emb // parts // LANES)
    width = (full // 2 + 15) // 16 * 16
    half = (parts, n_blk, width, LANES)
    steps = [pltpu.VMEM((parts, n_blk >> (s + 1), width, LANES), jnp.bfloat16) for s in range(4)]
    dma = pltpu.SemaphoreType.DMA
    loss, head_grad = pl.pallas_call(
        functools.partial(kernel, n_blk),
        out_shape=(
            jax.ShapeDtypeStruct((1, tok), jnp.float32),
            jax.ShapeDtypeStruct((depth, emb), jnp.float32),
        ),
        in_specs=[pl.BlockSpec(memory_space=pl.ANY)] * 3,
        out_specs=(pl.BlockSpec(memory_space=pltpu.VMEM),) * 2,
        scratch_shapes=[
            pltpu.VMEM((tok, emb), jnp.bfloat16),
            pltpu.VMEM((feat, emb), jnp.bfloat16),
            pltpu.VMEM((tok, emb), jnp.bfloat16),
            pltpu.VMEM((STEPS + 1, tok, feat), jnp.bfloat16),
            pltpu.VMEM((feat, (STEPS + 1) * tok), jnp.bfloat16),
            pltpu.VMEM(((STEPS + 1) * tok, emb), jnp.bfloat16),
            pltpu.VMEM(half, jnp.float32),
            pltpu.VMEM(half, jnp.bfloat16),
            pltpu.VMEM(half, jnp.bfloat16),
            *steps,
            *steps,
            pltpu.VMEM((parts, width, LANES), jnp.float32),
            pltpu.VMEM((parts, width, LANES), jnp.float32),
            dma((3,)),
            dma((N_CHUNK,)),
            dma((N_CHUNK,)),
            dma((N_CHUNK,)),
            dma((N_CHUNK,)),
            dma((parts,)),
            dma((parts,)),
            dma((parts, 4)),
            dma((parts, 4)),
            dma,
            dma,
        ],
        compiler_params=pltpu.CompilerParams(
            collective_id=0, has_side_effects=True, vmem_limit_bytes=40 * 1024 * 1024
        ),
    )(image_emb, text_feats, text_head)
    return loss.reshape(tok), head_grad


def shifted(block, axis, distance):
    n = lax.axis_size(axis)
    return lax.ppermute(block, axis, [((i - distance) % n, i) for i in range(n)])


def general(image_emb, text_feats, text_head):
    images = unit_images(image_emb)
    feats = [text_feats] + [shifted(text_feats, "blk", k) for k in range(1, STEPS + 1)]
    met = [meet(images, f, text_head, k == 0) for k, f in enumerate(feats)]
    loss = sum(m[0] for m in met).reshape(-1)
    local_grad = jnp.einsum(
        "td,te->de",
        jnp.concatenate(feats, axis=0),
        jnp.concatenate([m[1] for m in met], axis=0),
        preferred_element_type=jnp.float32,
    )
    row_sums = lax.psum_scatter(local_grad, "blk", scatter_dimension=0, tiled=True)
    return loss, lax.psum(row_sums, "grp")


def solution(mesh):
    n_blk, n_grp = mesh.shape["blk"], mesh.shape["grp"]
    body = functools.partial(fused, n_blk) if (n_blk, n_grp) == (16, 2) else general
    return jax.shard_map(
        body,
        mesh=mesh,
        in_specs=(P(("blk", "grp"), None), P(("blk", "grp"), None), P()),
        out_specs=(P(("blk", "grp")), P("blk", None)),
        check_vma=False,
    )
```

time: 251 us -> 38.6 us (0.15)
  waiting for transfers between devices: 217 us -> 0 us
  Pallas kernels: 0 us -> 33.3 us
  between operations: 14.8 us -> 0.65 us
  matrix products: 5.82 us -> 0 us
  starting transfers between devices: 4.82 us -> 0 us
    unnamed x3 -> x0, waiting for transfers between devices: 141 us -> none
    ppermute x5 -> x0, waiting for transfers between devices: 58.5 us -> none  [shifted(): return lax.ppermute(block, axis, route)]
    pallas_call x0 -> x1, Pallas kernels: none -> 33.3 us  [fused(): pl.pallas_call(functools.partial(kernel, n_blk), out_shape=(jax.ShapeDtyp...]
    psum x1 -> x0, waiting for transfers between devices: 17.6 us -> none  [per_device(): head_grad = lax.psum(row_sums, 'grp')]
    dot_general x8 -> x0, matrix products: 5.82 us -> none  [the longest x1 2.3 us: per_device(): jnp.einsum('td,te->de', text_feats, grad_proj, preferred_element_type=jnp...]
    ppermute x5 -> x0, starting transfers between devices: 4.74 us -> none  [shifted(): return lax.ppermute(block, axis, route)]
    unnamed x11 -> x8, local copies, waits for them, and re-layouts: 6.17 us -> 4.43 us
  transfers between devices with their start and end apart: 7 -> 0, of which waited for: 6 -> 0; matrix products, arithmetic and copies ran while one was open for 1% -> 0% of each run, Pallas kernels for 0% -> 0%
where the time goes in v1:
time: 38.6 us; the launch traced here: 38.4 us
  Pallas kernels  33.3 us (86%)
  local copies, waits for them, and re-layouts  4.43 us (11%)
  between operations  0.65 us (2%)
    pallas_call x1, Pallas kernels, fused(): pl.pallas_call(functools.partial(kernel, n_blk), out_shape=(jax.ShapeDtyp...  33.3 us
    unnamed x8, local copies, waits for them, and re-layouts  4.43 us

profile of v1, /device:TPU:0, one launch (start us, length us, event | category | flops | bytes accessed | tf_op | source)
XLA Modules:
  0.0 38.4 jit_solution(4399585072593466641)
XLA Ops:
  0.6 0.0 copy-start
  0.6 1.4 %copy-done = bf16[640,1152]{1,0:T(8,128)(2,1)S(1)} copy-done((bf16[640,1152]{1,0:T(8,128)(2,1)S(1)}, bf16[640,1152]{1,0:T(8,128)(2,1)}, u32[]{:S(2)}) %copy-start) | copy-done | bytes 1474584
  2.0 0.0 copy-start.1
  2.0 1.0 %copy-done.1 = bf16[128,1152]{1,0:T(8,128)(2,1)S(1)} copy-done((bf16[128,1152]{1,0:T(8,128)(2,1)S(1)}, bf16[128,1152]{1,0:T(8,128)(2,1)}, u32[]{:S(2)}) %copy-start.1) | copy-done | bytes 294936
  3.0 0.0 copy-start.2
  3.0 0.9 %copy-done.2 = bf16[128,640]{1,0:T(8,128)(2,1)S(1)} copy-done((bf16[128,640]{1,0:T(8,128)(2,1)S(1)}, bf16[128,640]{1,0:T(8,128)(2,1)}, u32[]{:S(2)}) %copy-start.2) | copy-done | bytes 163864
  3.9 33.3 %shard_map.50 = (f32[1,128]{1,0:T(1,128)S(1)}, f32[40,1152]{1,0:T(8,128)S(1)}) custom-call(bf16[128,1152]{1,0:T(8,128)(2,1)S(1)} %copy-done.1, bf16[128,640]{1,0:T(8,128)(2,1)S(1)} %copy-done.2, bf16[640,1152]{1,0:T(8,128)(2,1)S(1)} %copy-done), custom_call_target="tpu_custom_call" | custom-call | tf_op jit(solution)/shard_map/pallas_call | solution.py:242
  37.2 0.5 %copy.7 = f32[128]{0:T(128)} copy(f32[128]{0:T(128)S(1)} %bitcast.1) | data formatting | bytes 1024
  37.7 0.7 %copy.8 = f32[40,1152]{1,0:T(8,128)} copy(f32[40,1152]{1,0:T(8,128)S(1)} %get-tuple-element.9) | data formatting | bytes 368640
Async XLA Ops:
  0.6 1.4 %copy-start = (bf16[640,1152]{1,0:T(8,128)(2,1)S(1)}, bf16[640,1152]{1,0:T(8,128)(2,1)}, u32[]{:S(2)}) copy-start(bf16[640,1152]{1,0:T(8,128)(2,1)} %head_hbm.1) | copy-start | bytes 4423684
  2.0 1.0 %copy-start.1 = (bf16[128,1152]{1,0:T(8,128)(2,1)S(1)}, bf16[128,1152]{1,0:T(8,128)(2,1)}, u32[]{:S(2)}) copy-start(bf16[128,1152]{1,0:T(8,128)(2,1)} %image_hbm.1) | copy-start | bytes 884740
  3.0 0.9 %copy-start.2 = (bf16[128,640]{1,0:T(8,128)(2,1)S(1)}, bf16[128,640]{1,0:T(8,128)(2,1)}, u32[]{:S(2)}) copy-start(bf16[128,640]{1,0:T(8,128)(2,1)} %feats_hbm.1) | copy-start | bytes 491524

commit v2 on v1

--- a/solution.py
+++ b/solution.py
@@ -16,7 +16,10 @@
 
 LANES = 128
 N_CHUNK = 4
-ORDERS = ((0, 1, 2, 3), (1, 2, 0, 3), (2, 0, 1, 3))
+STAGES = (((0, 1), (2, 3)), ((0, 1), (2, 3)), ((2, 3), (0, 1)))
+ORDERS = tuple(sum(groups, ()) for groups in STAGES)
+SUB = 1
+CHAINS = SUB * len(ORDERS)
 
 
 def position(order, dest):
@@ -65,7 +68,7 @@
 def kernel(
     n_blk, image_hbm, feats_hbm, head_hbm, loss_ref, out_ref,
     image_v, head_v, units, feats, feats_t, grads, total, core_out, core_in,
-    out0, out1, out2, out3, in0, in1, in2, in3, mine, theirs,
+    out0, out1, in0, in1, mine, theirs,
     load_sem, s1, r1, s2, r2, core_s, core_r, step_s, step_r, last_s, last_r,
 ):
     blk, grp = lax.axis_index("blk"), lax.axis_index("grp")
@@ -79,7 +82,25 @@
     ahead = (lax.rem(blk + 2, n_blk), grp)
     behind = (lax.rem(blk + n_blk - 2, n_blk), grp)
     other = (blk, 1 - grp)
-    partners = [(flipped(bit), grp) for bit in range(4)]
+
+    def bit_of(bit):
+        return lax.rem(blk // (1 << bit), 2)
+
+    def partner(group, mask):
+        at = blk
+        for n, bit in enumerate(group):
+            if (mask >> n) % 2:
+                at = at + (1 << bit) * (1 - 2 * bit_of(bit))
+        return at, grp
+
+    def share(group, mask):
+        place = 0
+        for n, bit in enumerate(group):
+            value = bit_of(bit)
+            place = 2 * place + (1 - value if (mask >> n) % 2 else value)
+        return place
+
+    partners = [partner(group, mask) for group in sorted({g for p in STAGES for g in p}) for mask in range(1, 1 << len(group))]
 
     loads = [
         pltpu.make_async_copy(src, dst, load_sem.at[n])
@@ -146,14 +167,15 @@
     loss_ref[...] = loss + block(1)
 
     depth = out_ref.shape[0]
-    width = total.shape[2]
+    short = total.shape[2]
+    width = SUB * short
     columns = out_ref.shape[1] // len(ORDERS)
     tiles = columns // LANES
     full = depth * tiles
     first = grp == 0
 
     core_copies = [
-        remote(core_out.at[p], core_in.at[p], core_s.at[p], core_r.at[p], other) for p in range(len(ORDERS))
+        remote(core_out.at[q], core_in.at[q], core_s.at[q], core_r.at[q], other) for q in range(CHAINS)
     ]
 
     def products(p):
@@ -165,51 +187,71 @@
             stack = jnp.concatenate([piece[:, t * LANES : (t + 1) * LANES] for t in range(tiles)], axis=0)
             low, high = stack[:width], stack[full - width :]
             at = position(ORDERS[p], dest)
-            total[p, at] = jnp.where(first, low, high)
-            core_out[p, at] = jnp.where(first, high, low).astype(jnp.bfloat16)
-        core_copies[p].start()
-
-    outs, ins = (out0, out1, out2, out3), (in0, in1, in2, in3)
-    step_copies = [
-        [
-            remote(outs[s].at[p], ins[s].at[p], step_s.at[p, s], step_r.at[p, s], partners[ORDERS[p][s]])
-            for s in range(4)
+            kept = jnp.where(first, low, high)
+            given = jnp.where(first, high, low).astype(jnp.bfloat16)
+            for u in range(SUB):
+                total[SUB * p + u, at] = kept[u * short : (u + 1) * short]
+                core_out[SUB * p + u, at] = given[u * short : (u + 1) * short]
+        for u in range(SUB):
+            core_copies[SUB * p + u].start()
+
+    outs, ins = (out0, out1), (in0, in1)
+
+    def messages(q, s):
+        group = STAGES[q // SUB][s]
+        return [
+            remote(
+                outs[s].at[q, m - 1], ins[s].at[q, m - 1],
+                step_s.at[q, s, m - 1], step_r.at[q, s, m - 1], partner(group, m),
+            )
+            for m in range(1, 1 << len(group))
         ]
-        for p in range(len(ORDERS))
-    ]
-    base = [0] * len(ORDERS)
-
-    def halve(p, s):
-        count = n_blk >> (s + 1)
-        bit = lax.rem(blk // (1 << ORDERS[p][s]), 2)
-        keep, give = base[p] + bit * count, base[p] + (1 - bit) * count
+
+    step_copies = [[messages(q, s) for s in range(2)] for q in range(CHAINS)]
+    base = [0] * CHAINS
+    count = [n_blk] * CHAINS
+
+    def exchange(q, s):
+        group = STAGES[q // SUB][s]
+        start, size = base[q], count[q] >> len(group)
         if s == 0:
-            core_copies[p].wait_recv()
-            arrived, start = core_in, 0
+            core_copies[q].wait_recv()
         else:
-            step_copies[p][s - 1].wait_recv()
-            arrived, start = ins[s - 1], base[p]
-        gone = pl.ds(give, count)
-        outs[s][p] = (total[p, gone] + arrived[p, pl.ds(give - start, count)].astype(jnp.float32)).astype(
-            jnp.bfloat16
-        )
-        step_copies[p][s].start()
-        stay = pl.ds(keep, count)
-        total[p, stay] = total[p, stay] + arrived[p, pl.ds(keep - start, count)].astype(jnp.float32)
-        base[p] = keep
+            for copy in step_copies[q][s - 1]:
+                copy.wait_recv()
+
+        def summed(at):
+            value = total[q, pl.ds(at, size)]
+            if s == 0:
+                return value + core_in[q, pl.ds(at, size)].astype(jnp.float32)
+            for m in range(ins[s - 1].shape[1]):
+                value = value + ins[s - 1][q, m, pl.ds(at - start, size)].astype(jnp.float32)
+            return value
+
+        for m, copy in reversed(list(enumerate(step_copies[q][s], 1))):
+            outs[s][q, m - 1] = summed(start + share(group, m) * size).astype(jnp.bfloat16)
+            copy.start()
+        keep = start + share(group, 0) * size
+        total[q, pl.ds(keep, size)] = summed(keep)
+        base[q], count[q] = keep, size
 
     products(0)
     products(1)
-    halve(0, 0)
+    for u in range(SUB):
+        exchange(u, 0)
     products(2)
-    halve(1, 0)
-    halve(2, 0)
-    for s in range(1, 4):
-        for p in range(len(ORDERS)):
-            halve(p, s)
-    for p in range(len(ORDERS)):
-        step_copies[p][3].wait_recv()
-        mine[p] = total[p, base[p]] + in3[p, 0].astype(jnp.float32)
+    for q in range(SUB, CHAINS):
+        exchange(q, 0)
+    for q in range(CHAINS):
+        exchange(q, 1)
+    for q in range(CHAINS):
+        for copy in step_copies[q][1]:
+            copy.wait_recv()
+        row = (q % SUB) * short
+        value = total[q, base[q]]
+        for m in range(in1.shape[1]):
+            value = value + in1[q, m, 0].astype(jnp.float32)
+        mine[q // SUB, row : row + short] = value
     last = remote(mine, theirs, last_s, last_r, other)
     last.start()
     last.wait_recv()
@@ -225,7 +267,7 @@
     for copy in far + near + core_copies:
         copy.wait_send()
     for chain in step_copies:
-        for copy in chain:
+        for copy in chain[0] + chain[1]:
             copy.wait_send()
 
 
@@ -235,9 +277,11 @@
     depth = feat // n_blk
     parts = len(ORDERS)
     full = depth * (emb // parts // LANES)
-    width = (full // 2 + 15) // 16 * 16
-    half = (parts, n_blk, width, LANES)
-    steps = [pltpu.VMEM((parts, n_blk >> (s + 1), width, LANES), jnp.bfloat16) for s in range(4)]
+    unit = 16 * SUB
+    width = (full // 2 + unit - 1) // unit * unit
+    short = width // SUB
+    half = (CHAINS, n_blk, short, LANES)
+    steps = [pltpu.VMEM((CHAINS, 3, n_blk >> (2 * s + 2), short, LANES), jnp.bfloat16) for s in range(2)]
     dma = pltpu.SemaphoreType.DMA
     loss, head_grad = pl.pallas_call(
         functools.partial(kernel, n_blk),
@@ -245,7 +289,7 @@
             jax.ShapeDtypeStruct((1, tok), jnp.float32),
             jax.ShapeDtypeStruct((depth, emb), jnp.float32),
         ),
-        in_specs=[pl.BlockSpec(memory_space=pl.ANY)] * 3,
+        in_specs=[pl.BlockSpec(memory_space=pltpu.HBM)] * 3,
         out_specs=(pl.BlockSpec(memory_space=pltpu.VMEM),) * 2,
         scratch_shapes=[
             pltpu.VMEM((tok, emb), jnp.bfloat16),
@@ -266,15 +310,15 @@
             dma((N_CHUNK,)),
             dma((N_CHUNK,)),
             dma((N_CHUNK,)),
-            dma((parts,)),
-            dma((parts,)),
-            dma((parts, 4)),
-            dma((parts, 4)),
+            dma((CHAINS,)),
+            dma((CHAINS,)),
+            dma((CHAINS, 2, 3)),
+            dma((CHAINS, 2, 3)),
             dma,
             dma,
         ],
         compiler_params=pltpu.CompilerParams(
-            collective_id=0, has_side_effects=True, vmem_limit_bytes=40 * 1024 * 1024
+            collective_id=0, has_side_effects=True, vmem_limit_bytes=63 * 1024 * 1024
         ),
     )(image_emb, text_feats, text_head)
     return loss.reshape(tok), head_grad

time: 38.6 us -> 35.3 us (0.915)
  local copies, waits for them, and re-layouts: 4.43 us -> 2.74 us
  Pallas kernels: 33.3 us -> 31.7 us
    unnamed x8 -> x2, local copies, waits for them, and re-layouts: 4.43 us -> 2.74 us
    pallas_call x1, Pallas kernels: 33.3 us -> 31.7 us  [fused(): pl.pallas_call(functools.partial(kernel, n_blk), out_shape=(jax.ShapeDtyp...]
where the time goes in v2:
time: 35.3 us; the launch traced here: 35.1 us
  Pallas kernels  31.7 us (90%)
  local copies, waits for them, and re-layouts  2.74 us (8%)
  between operations  0.64 us (2%)
    pallas_call x1, Pallas kernels, fused(): pl.pallas_call(functools.partial(kernel, n_blk), out_shape=(jax.ShapeDtyp...  31.7 us
    unnamed x2, local copies, waits for them, and re-layouts  2.74 us

profile of v2, /device:TPU:0, one launch (start us, length us, event | category | flops | bytes accessed | tf_op | source)
XLA Modules:
  0.0 35.1 jit_solution(6884361633154357958)
XLA Ops:
  0.6 31.7 %shard_map.50 = (f32[1,128]{1,0:T(1,128)}, f32[40,1152]{1,0:T(8,128)}) custom-call(bf16[128,1152]{1,0:T(8,128)(2,1)} %image_hbm.1, bf16[128,640]{1,0:T(8,128)(2,1)} %feats_hbm.1, bf16[640,1152]{1,0:T(8,128)(2,1)} %head_hbm.1), custom_call_target="tpu_custom_call" | custom-call | tf_op jit(solution)/shard_map/pallas_call | solution.py:286
  32.4 1.1 %copy.7 = f32[128]{0:T(128)} copy(f32[128]{0:T(128)} %bitcast.1) | data formatting | bytes 1024
  33.5 1.6 %copy.8 = f32[40,1152]{1,0:T(8,128)} copy(f32[40,1152]{1,0:T(8,128)} %get-tuple-element.9) | data formatting | bytes 368640

commit v3 on v2

--- a/solution.py
+++ b/solution.py
@@ -67,7 +67,7 @@
 
 def kernel(
     n_blk, image_hbm, feats_hbm, head_hbm, loss_ref, out_ref,
-    image_v, head_v, units, feats, feats_t, grads, total, core_out, core_in,
+    image_v, head_v, units, feats, feats_t, grads, early, total, core_out, core_in,
     out0, out1, in0, in1, mine, theirs,
     load_sem, s1, r1, s2, r2, core_s, core_r, step_s, step_r, last_s, last_r,
 ):
@@ -148,8 +148,9 @@
 
     def block(k):
         loss, grad = meet(units[...], feats[k], head_v[...], k == 0)
-        grads[k * tok : (k + 1) * tok, :] = grad
-        feats_t[:, k * tok : (k + 1) * tok] = feats[k].T
+        at = (0, 2, 1)[k]
+        grads[at * tok : (at + 1) * tok, :] = grad
+        feats_t[:, at * tok : (at + 1) * tok] = feats[k].T
         return loss
 
     loss = block(0)
@@ -162,6 +163,7 @@
             onward[c].start()
 
     loss = loss + block(2)
+    early[...] = jnp.dot(feats_t[:, : 2 * tok], grads[: 2 * tok], preferred_element_type=jnp.float32)
     for copy in near:
         copy.wait_recv()
     loss_ref[...] = loss + block(1)
@@ -179,8 +181,9 @@
     ]
 
     def products(p):
-        grad = jnp.dot(
-            feats_t[...], grads[:, p * columns : (p + 1) * columns], preferred_element_type=jnp.float32
+        span = slice(p * columns, (p + 1) * columns)
+        grad = early[:, span] + jnp.dot(
+            feats_t[:, 2 * tok :], grads[2 * tok :, span], preferred_element_type=jnp.float32
         )
         for dest in range(n_blk):
             piece = grad[dest * depth : (dest + 1) * depth]
@@ -298,6 +301,7 @@
             pltpu.VMEM((STEPS + 1, tok, feat), jnp.bfloat16),
             pltpu.VMEM((feat, (STEPS + 1) * tok), jnp.bfloat16),
             pltpu.VMEM(((STEPS + 1) * tok, emb), jnp.bfloat16),
+            pltpu.VMEM((feat, emb), jnp.float32),
             pltpu.VMEM(half, jnp.float32),
             pltpu.VMEM(half, jnp.bfloat16),
             pltpu.VMEM(half, jnp.bfloat16),
@@ -318,7 +322,7 @@
             dma,
         ],
         compiler_params=pltpu.CompilerParams(
-            collective_id=0, has_side_effects=True, vmem_limit_bytes=63 * 1024 * 1024
+            collective_id=0, has_side_effects=True, vmem_limit_bytes=54784 * 1024
         ),
     )(image_emb, text_feats, text_head)
     return loss.reshape(tok), head_grad

time: 35.3 us -> 33.4 us (0.946)
  Pallas kernels: 31.7 us -> 30.3 us
  local copies, waits for them, and re-layouts: 2.74 us -> 2.09 us
    pallas_call x1, Pallas kernels: 31.7 us -> 30.3 us  [fused(): pl.pallas_call(functools.partial(kernel, n_blk), out_shape=(jax.ShapeDtyp...]
    unnamed x2 -> x4, local copies, waits for them, and re-layouts: 2.74 us -> 2.09 us
where the time goes in v3:
time: 33.4 us; the launch traced here: 33.1 us
  Pallas kernels  30.3 us (91%)
  local copies, waits for them, and re-layouts  2.09 us (6%)
  between operations  0.65 us (2%)
    pallas_call x1, Pallas kernels, fused(): pl.pallas_call(functools.partial(kernel, n_blk), out_shape=(jax.ShapeDtyp...  30.3 us
    unnamed x4, local copies, waits for them, and re-layouts  2.09 us

profile of v3, /device:TPU:0, one launch (start us, length us, event | category | flops | bytes accessed | tf_op | source)
XLA Modules:
  0.0 33.1 jit_solution(6822091372711474387)
XLA Ops:
  0.6 0.0 copy-start
  0.6 0.9 %copy-done = bf16[128,640]{1,0:T(8,128)(2,1)S(1)} copy-done((bf16[128,640]{1,0:T(8,128)(2,1)S(1)}, bf16[128,640]{1,0:T(8,128)(2,1)}, u32[]{:S(2)}) %copy-start) | copy-done | bytes 163864
  1.5 30.3 %shard_map.50 = (f32[1,128]{1,0:T(1,128)S(1)}, f32[40,1152]{1,0:T(8,128)S(1)}) custom-call(bf16[128,1152]{1,0:T(8,128)(2,1)} %image_hbm.1, bf16[128,640]{1,0:T(8,128)(2,1)S(1)} %copy-done, bf16[640,1152]{1,0:T(8,128)(2,1)} %head_hbm.1), custom_call_target="tpu_custom_call" | custom-call | tf_op jit(solution)/shard_map/pallas_call | solution.py:289
  31.9 0.5 %copy.7 = f32[128]{0:T(128)} copy(f32[128]{0:T(128)S(1)} %bitcast.1) | data formatting | bytes 1024
  32.4 0.7 %copy.8 = f32[40,1152]{1,0:T(8,128)} copy(f32[40,1152]{1,0:T(8,128)S(1)} %get-tuple-element.9) | data formatting | bytes 368640
Async XLA Ops:
  0.6 0.9 %copy-start = (bf16[128,640]{1,0:T(8,128)(2,1)S(1)}, bf16[128,640]{1,0:T(8,128)(2,1)}, u32[]{:S(2)}) copy-start(bf16[128,640]{1,0:T(8,128)(2,1)} %feats_hbm.1) | copy-start | bytes 491524

commit v4 on v3

--- a/solution.py
+++ b/solution.py
@@ -238,12 +238,14 @@
         total[q, pl.ds(keep, size)] = summed(keep)
         base[q], count[q] = keep, size
 
+    products(2)
     products(0)
     products(1)
     for u in range(SUB):
+        exchange(2 * SUB + u, 0)
+    for u in range(SUB):
         exchange(u, 0)
-    products(2)
-    for q in range(SUB, CHAINS):
+    for q in range(SUB, 2 * SUB):
         exchange(q, 0)
     for q in range(CHAINS):
         exchange(q, 1)

time: 33.4 us -> 32.3 us (0.967)
  Pallas kernels: 30.3 us -> 29.4 us
    pallas_call x1, Pallas kernels: 30.3 us -> 29.4 us  [fused(): pl.pallas_call(functools.partial(kernel, n_blk), out_shape=(jax.ShapeDtyp...]
where the time goes in v4:
time: 32.3 us; the launch traced here: 32.2 us
  Pallas kernels  29.4 us (91%)
  local copies, waits for them, and re-layouts  2.09 us (6%)
  between operations  0.65 us (2%)
    pallas_call x1, Pallas kernels, fused(): pl.pallas_call(functools.partial(kernel, n_blk), out_shape=(jax.ShapeDtyp...  29.4 us
    unnamed x4, local copies, waits for them, and re-layouts  2.09 us

profile of v4, /device:TPU:0, one launch (start us, length us, event | category | flops | bytes accessed | tf_op | source)
XLA Modules:
  0.0 32.2 jit_solution(11128612127310919609)
XLA Ops:
  0.6 0.0 copy-start
  0.6 0.9 %copy-done = bf16[128,640]{1,0:T(8,128)(2,1)S(1)} copy-done((bf16[128,640]{1,0:T(8,128)(2,1)S(1)}, bf16[128,640]{1,0:T(8,128)(2,1)}, u32[]{:S(2)}) %copy-start) | copy-done | bytes 163864
  1.5 29.4 %shard_map.50 = (f32[1,128]{1,0:T(1,128)S(1)}, f32[40,1152]{1,0:T(8,128)S(1)}) custom-call(bf16[128,1152]{1,0:T(8,128)(2,1)} %image_hbm.1, bf16[128,640]{1,0:T(8,128)(2,1)S(1)} %copy-done, bf16[640,1152]{1,0:T(8,128)(2,1)} %head_hbm.1), custom_call_target="tpu_custom_call" | custom-call | tf_op jit(solution)/shard_map/pallas_call | solution.py:291
  31.0 0.5 %copy.7 = f32[128]{0:T(128)} copy(f32[128]{0:T(128)S(1)} %bitcast.1) | data formatting | bytes 1024
  31.5 0.7 %copy.8 = f32[40,1152]{1,0:T(8,128)} copy(f32[40,1152]{1,0:T(8,128)S(1)} %get-tuple-element.9) | data formatting | bytes 368640
Async XLA Ops:
  0.6 0.9 %copy-start = (bf16[128,640]{1,0:T(8,128)(2,1)S(1)}, bf16[128,640]{1,0:T(8,128)(2,1)}, u32[]{:S(2)}) copy-start(bf16[128,640]{1,0:T(8,128)(2,1)} %feats_hbm.1) | copy-start | bytes 491524

commit v5 on v4

--- a/solution.py
+++ b/solution.py
@@ -240,9 +240,9 @@
 
     products(2)
     products(0)
-    products(1)
     for u in range(SUB):
         exchange(2 * SUB + u, 0)
+    products(1)
     for u in range(SUB):
         exchange(u, 0)
     for q in range(SUB, 2 * SUB):

time: 32.3 us -> 32.3 us (level)
  no operation moved by 1% of the time
where the time goes in v5:
time: 32.3 us; the launch traced here: 32.1 us
  Pallas kernels  29.4 us (91%)
  local copies, waits for them, and re-layouts  2.09 us (6%)
  between operations  0.65 us (2%)
    pallas_call x1, Pallas kernels, fused(): pl.pallas_call(functools.partial(kernel, n_blk), out_shape=(jax.ShapeDtyp...  29.4 us
    unnamed x4, local copies, waits for them, and re-layouts  2.09 us

profile of v5, /device:TPU:0, one launch (start us, length us, event | category | flops | bytes accessed | tf_op | source)
XLA Modules:
  0.0 32.1 jit_solution(17498612526148521780)
XLA Ops:
  0.6 0.0 copy-start
  0.6 0.9 %copy-done = bf16[128,640]{1,0:T(8,128)(2,1)S(1)} copy-done((bf16[128,640]{1,0:T(8,128)(2,1)S(1)}, bf16[128,640]{1,0:T(8,128)(2,1)}, u32[]{:S(2)}) %copy-start) | copy-done | bytes 163864
  1.5 29.4 %shard_map.50 = (f32[1,128]{1,0:T(1,128)S(1)}, f32[40,1152]{1,0:T(8,128)S(1)}) custom-call(bf16[128,1152]{1,0:T(8,128)(2,1)} %image_hbm.1, bf16[128,640]{1,0:T(8,128)(2,1)S(1)} %copy-done, bf16[640,1152]{1,0:T(8,128)(2,1)} %head_hbm.1), custom_call_target="tpu_custom_call" | custom-call | tf_op jit(solution)/shard_map/pallas_call | solution.py:291
  31.0 0.5 %copy.7 = f32[128]{0:T(128)} copy(f32[128]{0:T(128)S(1)} %bitcast.1) | data formatting | bytes 1024
  31.5 0.7 %copy.8 = f32[40,1152]{1,0:T(8,128)} copy(f32[40,1152]{1,0:T(8,128)S(1)} %get-tuple-element.9) | data formatting | bytes 368640
Async XLA Ops:
  0.6 0.9 %copy-start = (bf16[128,640]{1,0:T(8,128)(2,1)S(1)}, bf16[128,640]{1,0:T(8,128)(2,1)}, u32[]{:S(2)}) copy-start(bf16[128,640]{1,0:T(8,128)(2,1)} %feats_hbm.1) | copy-start | bytes 491524
